TPU v7x, 256 devices: a whole 4x4x8 slice. The times are simulated.
256 devices in a mesh: ctx: 32 (over y, x, z_hi), head: 8 (over z_lo, core).
Axes of the slice: x: 4, y: 4, z: 8 (z_hi: 2, z_lo: 4; z = z_hi * 4 + z_lo), core: 2. Of those that a mesh axis runs over, the one named last changes fastest.
Arguments:
- compressed: bfloat16 [6144, 576], P('ctx'), may hold values from -40 to 40
- query: bfloat16 [6144, 128, 192], P('ctx', 'head'), may hold values from -100 to 100
- d_output: bfloat16 [6144, 128, 128], P('ctx', 'head'), may hold values from -6 to 6
- w_uk: bfloat16 [512, 128, 128], P(None, 'head'), may hold values from -0.25 to 0.25
- w_uv: bfloat16 [512, 128, 128], P(None, 'head'), may hold values from -0.25 to 0.25
Outputs:
- d_query: float32 [6144, 128, 192], P('ctx', 'head')
- d_compressed: float32 [6144, 576], P(('ctx', 'head'))
- d_w_uk: float32 [512, 128, 128], P('ctx', 'head')
- d_w_uv: float32 [512, 128, 128], P('ctx', 'head')
All inputs are finite; a program needn't handle non-finite values.
Results may differ from a plain program's by a relative error of at most 0.012.
Values may be sent and summed in bfloat16 or wider, within the bound.
A program may use at most 128 MiB of HBM per device.

v0:
```python
import math

import jax
import jax.numpy as jnp
from jax import lax
from jax.sharding import Mesh
from jax.sharding import PartitionSpec as P

GROUP = 4
CTX = ("ctx_0", "ctx_1", "ctx_2")
CTX_HEAD = ("ctx_0", "ctx_1", "ctx_2", "head")


def partner(value, axis, apart):
    return lax.ppermute(value, axis, [(i, i ^ 1 << apart) for i in range(lax.axis_size(axis))])


def split_up(value, dim, peers):
    before, after = (value.shape[:dim], value.shape[dim + 1 :])
    return jnp.moveaxis(value.reshape(*before, peers, -1, *after), dim, 0)


def sum_at_owner(value, axis, dim):
    blocks = split_up(value, dim, lax.axis_size(axis))
    arrived = lax.all_to_all(blocks, axis, split_axis=0, concat_axis=0, tiled=True)
    return arrived.astype(jnp.float32).sum(axis=0)


def summed_rows(terms, axes):
    total = terms.astype(jnp.bfloat16)
    for axis in axes:
        total = lax.psum_scatter(total, axis, scatter_dimension=0, tiled=True)
    return total.astype(jnp.float32)


def split_halves(stacked, upper_half):
    half_rows = stacked.shape[1] // 2
    kept_part = jnp.where(upper_half, stacked[:, half_rows:], stacked[:, :half_rows])
    outgoing = jnp.where(upper_half, stacked[:, :half_rows], stacked[:, half_rows:])
    return (kept_part, outgoing)


def per_device(compressed, query, d_output, w_uk, w_uv):
    rows_own = compressed.shape[0]
    latent_width = w_uk.shape[0]
    heads_here = w_uk.shape[1]
    nope_width = w_uk.shape[2]
    value_width = w_uv.shape[2]
    score_scale = 1.0 / math.sqrt(query.shape[2])
    levels = GROUP.bit_length() - 1
    position = lax.axis_index(CTX)
    gathered = compressed
    for bit_index in range(levels):
        partner_rows = partner(gathered, CTX, bit_index)
        upper_half = position >> bit_index & 1 == 1
        gathered = jnp.concatenate(
            [
                jnp.where(upper_half, partner_rows, gathered),
                jnp.where(upper_half, gathered, partner_rows),
            ],
            axis=0,
        )
    span_rows = gathered.shape[0]
    latent = gathered[:, :latent_width]
    key_rope = gathered[:, latent_width:]
    weights = jnp.concatenate(
        [w_uk.reshape(latent_width, -1), w_uv.reshape(latent_width, -1)], axis=1
    )
    expanded = jnp.dot(latent, weights, preferred_element_type=jnp.float32).astype(jnp.bfloat16)
    split_at = heads_here * nope_width
    key_nope = expanded[:, :split_at].reshape(span_rows, heads_here, nope_width)
    values_here = expanded[:, split_at:].reshape(span_rows, heads_here, value_width)
    query_nope = query[..., :nope_width]
    query_rope = query[..., nope_width:]
    scores = jnp.einsum("ihd,jhd->hij", query_nope, key_nope, preferred_element_type=jnp.float32)
    scores = (
        scores + jnp.einsum("ihr,jr->hij", query_rope, key_rope, preferred_element_type=jnp.float32)
    ) * score_scale
    probs = jax.nn.softmax(scores, axis=-1)
    probs_low = probs.astype(jnp.bfloat16)
    attended = jnp.einsum(
        "hij,jhd->ihd", probs_low, values_here, preferred_element_type=jnp.float32
    )
    row_delta = jnp.sum(d_output.astype(jnp.float32) * attended, axis=-1)
    grad_probs = jnp.einsum(
        "ihd,jhd->hij", d_output, values_here, preferred_element_type=jnp.float32
    )
    score_grads = probs * (grad_probs - jnp.transpose(row_delta)[:, :, None])
    score_low = score_grads.astype(jnp.bfloat16)
    grad_nope = jnp.einsum("hij,jhd->ihd", score_low, key_nope, preferred_element_type=jnp.float32)
    grad_rope = jnp.einsum("hij,jr->ihr", score_low, key_rope, preferred_element_type=jnp.float32)
    d_query = jnp.concatenate([grad_nope, grad_rope], axis=-1) * score_scale
    key_grad = (
        jnp.einsum("hij,ihd->jhd", score_low, query_nope, preferred_element_type=jnp.float32)
        * score_scale
    ).astype(jnp.bfloat16)
    value_grad = jnp.einsum(
        "hij,ihd->jhd", probs_low, d_output, preferred_element_type=jnp.float32
    ).astype(jnp.bfloat16)
    rope_grad = (
        jnp.einsum("hij,ihr->jr", score_low, query_rope, preferred_element_type=jnp.float32)
        * score_scale
    )
    key_value = jnp.concatenate(
        [key_grad.reshape(span_rows, -1), value_grad.reshape(span_rows, -1)], axis=1
    )
    latent_grad = lax.dot_general(
        key_value, weights, (((1,), (1,)), ((), ())), preferred_element_type=jnp.float32
    )
    partial_value = jnp.concatenate([latent_grad, rope_grad], axis=1)
    column_count = partial_value.shape[1]
    head_count = lax.axis_size("head")
    share_rows = rows_own // head_count
    shares = partial_value.reshape(GROUP, head_count, share_rows, column_count)
    shares = jnp.transpose(shares, (1, 0, 2, 3)).reshape(-1, column_count)
    shares = sum_at_owner(shares.astype(jnp.bfloat16), "head", 0)
    stacked = shares.reshape(GROUP, share_rows, column_count)[None]
    for bit_index in reversed(range(levels)):
        upper_half = position >> bit_index & 1 == 1
        kept_part, outgoing = split_halves(stacked, upper_half)
        incoming = partner(outgoing, CTX, bit_index)
        stacked = kept_part + incoming
    d_compressed = stacked[0, 0]
    rows_each = latent_width // lax.axis_size(CTX)
    summed = summed_rows(
        lax.dot_general(
            latent, key_value, (((0,), (0,)), ((), ())), preferred_element_type=jnp.float32
        ),
        CTX,
    )
    d_w_uk = summed[:, :split_at].reshape(rows_each, heads_here, nope_width)
    d_w_uv = summed[:, split_at:].reshape(rows_each, heads_here, value_width)
    return (d_query, d_compressed, d_w_uk, d_w_uv)


def solution(mesh):
    torus = Mesh(
        mesh.devices.reshape(4, 4, 2, mesh.shape["head"]), ("ctx_0", "ctx_1", "ctx_2", "head")
    )
    placed = (
        P(CTX, None),
        P(CTX, "head", None),
        P(CTX, "head", None),
        P(None, "head", None),
        P(None, "head", None),
    )
    return jax.shard_map(
        per_device,
        mesh=torus,
        in_specs=placed,
        out_specs=(
            P(CTX, "head", None),
            P(CTX_HEAD, None),
            P(CTX, "head", None),
            P(CTX, "head", None),
        ),
        check_vma=False,
    )
```

profile of v0, /device:TPU:32, one launch (start us, length us, event | category | flops | bytes accessed | tf_op | source)
XLA Modules:
  0.0 206.8 jit_solution(16629641493890031727)
XLA Ops:
  7.2 1.2 copy.23
  8.5 6.4 %collective-permute-start = (bf16[192,576]{0,1:T(8,128)(2,1)S(1)}, bf16[192,576]{0,1:T(8,128)(2,1)S(1)}, u32[]{:S(2)}, u32[]{:S(2)}) collective-permute-start(bf16[192,576]{0,1:T(8,128)(2,1)S(1)} %copy.23), channel_id=1, source_target_pairs={{0,8},{8,0},{16,24},{24,16},{32,40},{40,32},{48,56},{56,48},{64,72... | collective-permute-start | bytes 663560 | tf_op jit(solution)/shard_map/ppermute | solution.py:15
  14.9 3.5 %bitcast_dynamic-update-slice_fusion.1 = bf16[512,4096]{1,0:T(8,128)(2,1)} fusion(bf16[64,8,16,128]{3,2,1,0:T(8,128)(2,1)} %bitcast.100), kind=kLoop, calls=%fused_computation.30 | loop fusion | bytes 4194304
  19.4 1.4 copy.41
  20.9 7.4 %collective-permute-done = bf16[192,576]{0,1:T(8,128)(2,1)S(1)} collective-permute-done((bf16[192,576]{0,1:T(8,128)(2,1)S(1)}, bf16[192,576]{0,1:T(8,128)(2,1)S(1)}, u32[]{:S(2)}, u32[]{:S(2)}) %collective-permute-start) | collective-permute-done | bytes 221216 | tf_op jit(solution)/shard_map/ppermute | solution.py:15
  28.5 1.6 collective-permute-start.1
  30.1 3.5 %bitcast_dynamic-update-slice_fusion = bf16[512,4096]{1,0:T(8,128)(2,1)} fusion(bf16[512,4096]{1,0:T(8,128)(2,1)} %bitcast_dynamic-update-slice_fusion.1, bf16[64,8,16,128]{3,2,1,0:T(8,128)(2,1)} %bitcast.101), kind=kLoop, calls=%fused_computation.29 | loop fusion | bytes 4194304 | tf_op jit(solution)/shard_map/concatenate | solution.py:66
  33.6 6.3 %collective-permute-done.1 = bf16[384,576]{0,1:T(8,128)(2,1)S(1)} collective-permute-done((bf16[384,576]{0,1:T(8,128)(2,1)S(1)}, bf16[384,576]{0,1:T(8,128)(2,1)S(1)}, u32[]{:S(2)}, u32[]{:S(2)}) %collective-permute-start.1) | collective-permute-done | bytes 442400 | tf_op jit(solution)/shard_map/ppermute | solution.py:15
  41.1 5.9 %convolution_convert_fusion = bf16[768,4096]{1,0:T(8,128)(2,1)S(1)} fusion(bf16[512,4096]{1,0:T(8,128)(2,1)} %bitcast_dynamic-update-slice_fusion, bf16[384,576]{0,1:T(8,128)(2,1)S(1)} %get-tuple-element.14, bf16[384,576]{0,1:T(8,128)(2,1)S(1)} %get-tuple-element.15), kind=kOutput, calls=%fused_computation.6 | convolution fusion | flops 3225944064 | bytes 11370496 | tf_op jit(solution)/shard_map/dot_general | solution.py:69
  47.1 3.7 %slice_bitcast_fusion = (bf16[96,16,8,128]{3,2,1,0:T(8,128)(2,1)}, bf16[96,16,8,128]{3,2,1,0:T(8,128)(2,1)S(1)}) fusion(bf16[768,4096]{1,0:T(8,128)(2,1)S(1)} %convolution_convert_fusion), kind=kLoop, calls=%fused_computation.21 | loop fusion | bytes 12582912
  50.8 5.1 %fusion.10 = f32[16,768,192]{1,2,0:T(8,128)} fusion(bf16[96,16,8,128]{3,2,1,0:T(8,128)(2,1)S(1)} %get-tuple-element.13, bf16[192,16,128]{2,1,0:T(8,128)(2,1)S(1)} %copy-done.1), kind=kOutput, calls=%fused_computation.17 | convolution fusion | flops 603979776 | bytes 13369344 | tf_op jit(solution)/shard_map/ihd,jhd->hij/dot_general | solution.py:75
  55.9 11.0 %fusion.40 = (f32[16,192]{1,0:T(8,128)S(1)}, f32[16,192,768]{2,1,0:T(8,128)}) fusion(f32[16,768,192]{1,2,0:T(8,128)} %fusion.10, bf16[768,64,1]{0,1,2:T(8,128)(2,1)S(1)} %fusion.34, bf16[192,16,64]{0,2,1:T(8,128)(2,1)} %copy.41), kind=kOutput, calls=%fused_computation.65 | convolution fusion | flops 311427840 | bytes 19378176 | tf_op jit(solution)/shard_map/sub | solution.py:79
  66.9 4.2 %fusion.4 = bf16[16,192,768]{2,1,0:T(8,128)(2,1)S(1)} fusion(f32[16,192,768]{2,1,0:T(8,128)} %get-tuple-element.21, f32[16,192]{1,0:T(8,128)S(1)} %get-tuple-element.20), kind=kLoop, calls=%fused_computation.12 | loop fusion | flops 4718592 | bytes 14168064 | tf_op jit(solution)/shard_map/convert_element_type | solution.py:80
  72.2 5.1 %fusion.18 = f32[192,16]{0,1:T(8,128)S(1)} fusion(bf16[16,192,768]{2,1,0:T(8,128)(2,1)S(1)} %fusion.4, bf16[96,16,8,128]{3,2,1,0:T(8,128)(2,1)} %get-tuple-element.12, bf16[192,16,128]{2,1,0:T(8,128)(2,1)S(1)} %copy-done.11), kind=kOutput, calls=%fused_computation.33 | convolution fusion | flops 605156352 | bytes 8663040 | tf_op jit(solution)/shard_map/hij,jhd->ihd/dot_general | solution.py:81
  77.4 4.0 %fusion.1 = bf16[16,192,768]{2,1,0:T(8,128)(2,1)S(1)} fusion(f32[16,192]{1,0:T(8,128)S(1)} %bitcast.106, f32[16,192,768]{2,1,0:T(8,128)S(1)} %bitcast.93, f32[16,192]{1,0:T(8,128)S(1)} %get-tuple-element.20, bf16[96,16,8,128]{3,2,1,0:T(8,128)(2,1)} %get-tuple-element.12, bf16[192,16,128]{2,1,0:T(8,128)(2,1)S(1)} %copy-done.11), kind=kOutput, calls=%fused_computation.2 | convolution fusion | flops 613416960 | bytes 18112512 | tf_op jit(solution)/shard_map/ihd,jhd->hij/dot_general | solution.py:85
  81.4 1.2 multiply_convert_fusion
  83.5 1.7 copy-done.12
  85.2 8.2 %convolution_convert_fusion.1 = bf16[512,4096]{1,0:T(8,128)(2,1)} fusion(bf16[768,2048]{0,1:T(8,128)(2,1)S(1)} %bitcast.96, bf16[768,2048]{0,1:T(8,128)(2,1)S(1)} %bitcast.104, bf16[384,576]{0,1:T(8,128)(2,1)S(1)} %copy-done.7, bf16[384,576]{0,1:T(8,128)(2,1)S(1)} %copy-done.9), kind=kOutput, calls=%fused_computation.9 | convolution fusion | flops 3237478400 | bytes 11370496 | tf_op jit(solution)/shard_map/dot_general | solution.py:126
  93.5 3.6 %fusion.26 = bf16[768,64]{0,1:T(8,128)(2,1)S(1)} fusion(bf16[192,16,64]{0,2,1:T(8,128)(2,1)} %copy.41, bf16[16,192,768]{2,1,0:T(8,128)(2,1)} %copy-done), kind=kOutput, calls=%fused_computation.39 | convolution fusion | flops 302088192 | bytes 5210112 | tf_op jit(solution)/shard_map/hij,ihr->jr/dot_general | solution.py:101
  97.1 6.6 %fusion.24 = bf16[768,512]{0,1:T(8,128)(2,1)S(1)} fusion(bf16[512,4096]{1,0:T(8,128)(2,1)} %bitcast_dynamic-update-slice_fusion, bf16[768,2048]{0,1:T(8,128)(2,1)S(1)} %bitcast.97, bf16[768,2048]{0,1:T(8,128)(2,1)} %bitcast.105), kind=kOutput, calls=%fused_computation.36 | convolution fusion | flops 3234201600 | bytes 11272192 | tf_op jit(solution)/shard_map/dot_general | solution.py:107
  104.7 2.2 %copy.36 = bf16[768,576]{1,0:T(8,128)(2,1)} copy(bf16[768,576]{0,1:T(8,128)(2,1)} %pad_maximum_fusion.5) | data formatting | bytes 1769472 | tf_op jit(solution)/shard_map/concatenate | solution.py:110
  106.9 2.3 %copy.37 = bf16[8,4,24,576]{3,2,1,0:T(8,128)(2,1)} copy(bf16[8,4,24,576]{3,2,0,1:T(8,128)(2,1)} %bitcast.94) | data formatting | bytes 1769472 | tf_op jit(solution)/shard_map/convert_element_type | solution.py:116
  109.2 4.2 %all-to-all-start = ((bf16[8,96,576]{2,1,0:T(8,128)(2,1)}), bf16[8,96,576]{2,1,0:T(8,128)(2,1)}, u32[]{:S(2)}, u32[]{:S(2)}) async-start(bf16[8,96,576]{2,1,0:T(8,128)(2,1)} %bitcast.95), calls=%async_computation | async-start | bytes 1966080 | tf_op jit(solution)/shard_map/all_to_all | solution.py:25
  113.4 30.8 %reduce-scatter.4.cloned.1.call-done = bf16[128,4096]{1,0:T(8,128)(2,1)} async-done(((bf16[512,4096]{1,0:T(8,128)(2,1)}), bf16[128,4096]{1,0:T(8,128)(2,1)}) %reduce-scatter.4.cloned.1.call-update) | async-done | bytes 1048592 | tf_op jit(solution)/shard_map/reduce_scatter | solution.py:32
  144.3 4.9 %fusion.19 = f32[192,16,128]{2,0,1:T(8,128)} fusion(bf16[16,192,768]{2,1,0:T(8,128)(2,1)} %copy-done, bf16[96,16,8,128]{3,2,1,0:T(8,128)(2,1)S(1)} %get-tuple-element.13), kind=kOutput, calls=%fused_computation.35 | convolution fusion | flops 603979776 | bytes 9437184 | tf_op jit(solution)/shard_map/hij,jhd->ihd/dot_general | solution.py:90
  149.1 1.5 convert_reduce_fusion
  150.7 1.8 collective-permute-start.2
  152.5 3.7 %convolution_bitcast_fusion = f32[192,16,64]{2,0,1:T(8,128)S(1)} fusion(bf16[768,64,1]{0,1,2:T(8,128)(2,1)S(1)} %fusion.34, bf16[16,192,768]{2,1,0:T(8,128)(2,1)} %copy-done), kind=kOutput, calls=%fused_computation.34 | convolution fusion | flops 301989888 | bytes 5603328 | tf_op jit(solution)/shard_map/hij,jr->ihr/dot_general | solution.py:91
  156.2 16.5 %reduce-scatter.6.cloned.1.call-done = bf16[32,4096]{1,0:T(8,128)(2,1)} async-done(((bf16[128,4096]{1,0:T(8,128)(2,1)}), bf16[32,4096]{1,0:T(8,128)(2,1)}) %reduce-scatter.6.cloned.1.call-update) | async-done | bytes 262160 | tf_op jit(solution)/shard_map/reduce_scatter | solution.py:32
  172.8 4.9 %collective-permute-start.3 = (f32[1,1,24,576]{3,2,1,0:T(8,128)S(1)}, f32[1,1,24,576]{3,2,1,0:T(8,128)S(1)}, u32[]{:S(2)}, u32[]{:S(2)}) collective-permute-start(f32[1,1,24,576]{3,2,1,0:T(8,128)S(1)} %slice_select_fusion.1), channel_id=1, source_target_pairs={{0,8},{8,0},{16,24},{24,16},{32,40},{40,32},{48,56},{56,48},{64,72... | collective-permute-start | bytes 165896 | tf_op jit(solution)/shard_map/ppermute | solution.py:15
  178.1 3.5 %copy.38 = f32[192,16,192]{2,1,0:T(8,128)} copy(f32[192,16,192]{2,0,1:T(8,128)S(1)} %maximum_multiply_fusion) | data formatting | bytes 4718592
  182.2 15.7 %reduce-scatter.8.cloned.1.call-done = bf16[16,4096]{1,0:T(8,128)(2,1)} async-done(((bf16[32,4096]{1,0:T(8,128)(2,1)}), bf16[16,4096]{1,0:T(8,128)(2,1)}) %reduce-scatter.8.cloned.1.call-update) | async-done | bytes 131088 | tf_op jit(solution)/shard_map/reduce_scatter | solution.py:32
  (59 shorter events, 9.1 us)
Async XLA Ops:
  7.2 11.2 %copy-start.5 = (bf16[192,16,192]{2,1,0:T(8,128)(2,1)S(1)}, bf16[192,16,192]{2,1,0:T(8,128)(2,1)}, u32[]{:S(2)}) copy-start(bf16[192,16,192]{2,1,0:T(8,128)(2,1)} %param.6) | copy-start | bytes 3538948
  7.2 12.3 %slice-start.3 = ((bf16[192,16,192]{2,1,0:T(8,128)(2,1)}), bf16[192,16,64]{2,1,0:T(8,128)(2,1)S(1)}, s32[]{:S(2)}) async-start(bf16[192,16,192]{2,1,0:T(8,128)(2,1)} %param.6), calls=%async_computation.10 | async-start | bytes 1572864 | tf_op jit(solution)/shard_map/slice | solution.py:74
  7.2 137.0 %reduce-scatter.4.cloned.1.call-start = ((), (), s32[]{:S(2)}) async-start(), calls=%async_computation.4 | async-start | bytes 5242880 | tf_op jit(solution)/shard_map/reduce_scatter | solution.py:32
  8.5 19.8 %collective-permute-start = (bf16[192,576]{0,1:T(8,128)(2,1)S(1)}, bf16[192,576]{0,1:T(8,128)(2,1)S(1)}, u32[]{:S(2)}, u32[]{:S(2)}) collective-permute-start(bf16[192,576]{0,1:T(8,128)(2,1)S(1)} %copy.23), channel_id=1, source_target_pairs={{0,8},{8,0},{16,24},{24,16},{32,40},{40,32},{48,56},{56,48},{64,72... | collective-permute-start | bytes 663560 | tf_op jit(solution)/shard_map/ppermute | solution.py:15
  28.5 11.4 %collective-permute-start.1 = (bf16[384,576]{0,1:T(8,128)(2,1)S(1)}, bf16[384,576]{0,1:T(8,128)(2,1)S(1)}, u32[]{:S(2)}, u32[]{:S(2)}) collective-permute-start(bf16[384,576]{0,1:T(8,128)(2,1)S(1)} %pad_maximum_fusion.6), channel_id=1, source_target_pairs={{0,16},{8,24},{16,0},{24,8},{32,48},{40,56},{48,32},{56,40},{64,80... | collective-permute-start | bytes 1327112 | tf_op jit(solution)/shard_map/ppermute | solution.py:15
  40.1 0.8 copy-start.6
  40.1 1.0 copy-start.8
  47.1 3.7 %copy-start.1 = (bf16[192,16,128]{2,1,0:T(8,128)(2,1)S(1)}, bf16[192,16,128]{2,1,0:T(8,128)(2,1)}, u32[]{:S(2)}) copy-start(bf16[192,16,128]{2,1,0:T(8,128)(2,1)} %slice.42) | copy-start | bytes 2359300
  66.9 4.2 %copy-start.11 = (bf16[192,16,128]{2,1,0:T(8,128)(2,1)S(1)}, bf16[192,16,128]{2,1,0:T(8,128)(2,1)}, u32[]{:S(2)}) copy-start(bf16[192,16,128]{2,1,0:T(8,128)(2,1)} %param.7) | copy-start | bytes 2359300
  71.1 6.2 %slice-start = ((s8[9437184]{0:T(1024)(128)(4,1)}), s8[4194304]{0:T(1024)(128)(4,1)S(1)}, s32[]{:S(2)}) async-start(s8[9437184]{0:T(1024)(128)(4,1)} %bitcast.92), calls=%async_computation.7 | async-start | bytes 8388608
  71.1 6.2 %slice-start.1 = ((s8[9437184]{0:T(1024)(128)(4,1)}), s8[4194304]{0:T(1024)(128)(4,1)S(1)}, s32[]{:S(2)}) async-start(s8[9437184]{0:T(1024)(128)(4,1)} %bitcast.92), calls=%async_computation.8 | async-start | bytes 8388608
  72.2 11.3 %copy-start.3 = (bf16[16,768,128]{1,2,0:T(8,128)(2,1)}, bf16[16,768,128]{1,2,0:T(8,128)(2,1)S(1)}, u32[]{:S(2)}) copy-start(bf16[16,768,128]{1,2,0:T(8,128)(2,1)S(1)} %convolution_convert_fusion.2) | copy-start | bytes 9437188
  72.2 5.2 %slice-start.2 = ((s8[9437184]{0:T(1024)(128)(4,1)}), s8[1048576]{0:T(1024)(128)(4,1)S(1)}, s32[]{:S(2)}) async-start(s8[9437184]{0:T(1024)(128)(4,1)} %bitcast.92), calls=%async_computation.9 | async-start | bytes 2097152
  77.4 4.0 %copy-start.2 = (bf16[192,16,128]{2,1,0:T(8,128)(2,1)S(1)}, bf16[192,16,128]{2,1,0:T(8,128)(2,1)}, u32[]{:S(2)}) copy-start(bf16[192,16,128]{2,1,0:T(8,128)(2,1)} %slice.42) | copy-start | bytes 2359300
  81.4 2.1 %copy-start = (bf16[16,192,768]{2,1,0:T(8,128)(2,1)}, bf16[16,192,768]{2,1,0:T(8,128)(2,1)S(1)}, u32[]{:S(2)}) copy-start(bf16[16,192,768]{2,1,0:T(8,128)(2,1)S(1)} %fusion.1) | copy-start | bytes 14155780
  81.4 3.8 %copy-start.7 = (bf16[384,576]{0,1:T(8,128)(2,1)S(1)}, bf16[384,576]{0,1:T(8,128)(2,1)}, u32[]{:S(2)}) copy-start(bf16[384,576]{0,1:T(8,128)(2,1)} %copy-done.6) | copy-start | bytes 1327108
  81.4 3.8 %copy-start.9 = (bf16[384,576]{0,1:T(8,128)(2,1)S(1)}, bf16[384,576]{0,1:T(8,128)(2,1)}, u32[]{:S(2)}) copy-start(bf16[384,576]{0,1:T(8,128)(2,1)} %copy-done.8) | copy-start | bytes 1327108
  83.5 1.7 copy-start.12
  93.4 3.6 %copy-start.4 = (bf16[16,768,128]{1,2,0:T(8,128)(2,1)S(1)}, bf16[16,768,128]{1,2,0:T(8,128)(2,1)}, u32[]{:S(2)}) copy-start(bf16[16,768,128]{1,2,0:T(8,128)(2,1)} %copy-done.3) | copy-start | bytes 9437188
  109.2 40.0 %all-to-all-start = ((bf16[8,96,576]{2,1,0:T(8,128)(2,1)}), bf16[8,96,576]{2,1,0:T(8,128)(2,1)}, u32[]{:S(2)}, u32[]{:S(2)}) async-start(bf16[8,96,576]{2,1,0:T(8,128)(2,1)} %bitcast.95), calls=%async_computation | async-start | bytes 1966080 | tf_op jit(solution)/shard_map/all_to_all | solution.py:25
  113.4 59.4 %reduce-scatter.6.cloned.1.call-start = ((), (), s32[]{:S(2)}) async-start(), calls=%async_computation.5 | async-start | bytes 1310720 | tf_op jit(solution)/shard_map/reduce_scatter | solution.py:32
  144.2 53.7 %reduce-scatter.8.cloned.1.call-start = ((), (), s32[]{:S(2)}) async-start(), calls=%async_computation.6 | async-start | bytes 393216 | tf_op jit(solution)/shard_map/reduce_scatter | solution.py:32
  149.1 28.5 %copy-start.10 = (f32[192,16,128]{2,0,1:T(8,128)S(1)}, f32[192,16,128]{2,0,1:T(8,128)}, u32[]{:S(2)}) copy-start(f32[192,16,128]{2,0,1:T(8,128)} %fusion.19) | copy-start | bytes 4718596
  150.7 5.5 %collective-permute-start.2 = (f32[1,2,24,576]{3,2,1,0:T(8,128)S(1)}, f32[1,2,24,576]{3,2,1,0:T(8,128)S(1)}, u32[]{:S(2)}, u32[]{:S(2)}) collective-permute-start(f32[1,2,24,576]{3,2,1,0:T(8,128)S(1)} %slice_select_fusion), channel_id=1, source_target_pairs={{0,16},{8,24},{16,0},{24,8},{32,48},{40,56},{48,32},{56,40},{64,80... | collective-permute-start | bytes 331784 | tf_op jit(solution)/shard_map/ppermute | solution.py:15
  172.8 8.8 %collective-permute-start.3 = (f32[1,1,24,576]{3,2,1,0:T(8,128)S(1)}, f32[1,1,24,576]{3,2,1,0:T(8,128)S(1)}, u32[]{:S(2)}, u32[]{:S(2)}) collective-permute-start(f32[1,1,24,576]{3,2,1,0:T(8,128)S(1)} %slice_select_fusion.1), channel_id=1, source_target_pairs={{0,8},{8,0},{16,24},{24,16},{32,40},{40,32},{48,56},{56,48},{64,72... | collective-permute-start | bytes 165896 | tf_op jit(solution)/shard_map/ppermute | solution.py:15
Sparse Core Ops, SparseCore 0:
  93.6 50.5 reduce-scatter.3
  146.9 25.8 reduce-scatter.5
  175.2 22.6 reduce-scatter.7
where the time goes:
time: 209 us; the launch traced here: 207 us
  waiting for transfers between devices  76.7 us (37%)
  matrix products  60.4 us (29%)
  local copies, waits for them, and re-layouts  27.5 us (13%)
  starting transfers between devices  19 us (9%)
  between operations  14.1 us (7%)
  other arithmetic  9.14 us (4%)
    reduce_scatter x3, waiting for transfers between devices, summed_rows(): total = lax.psum_scatter(total, axis, scatter_dimension=0, tiled=True)  63 us
    unnamed x40, local copies, waits for them, and re-layouts  18.4 us
    ppermute x4, starting transfers between devices, partner(): lax.ppermute(value, axis, [(i, i ^ 1 << apart) for i in range(lax.axis_si...  14.7 us
    ppermute x4, waiting for transfers between devices, partner(): lax.ppermute(value, axis, [(i, i ^ 1 << apart) for i in range(lax.axis_si...  13.7 us
    sub x1, matrix products, per_device(): probs = jax.nn.softmax(scores, axis=-1)  11 us
    dot_general x1, matrix products, per_device(): lax.dot_general(latent, key_value, (((0,), (0,)), ((), ())), preferred_el...  8.22 us
    dot_general x1, matrix products, per_device(): lax.dot_general(key_value, weights, (((1,), (1,)), ((), ())), preferred_e...  6.63 us
    dot_general x1, matrix products, per_device(): jnp.dot(latent, weights, preferred_element_type=jnp.float32)  5.95 us
  transfers between devices with their start and end apart: 8, of which 5 were waited for; matrix products, arithmetic and copies ran while one was open for 19% of the time, Pallas kernels for 0%

commit v1 on v0

v1 whole, which is shorter than its diff:
```python
import functools
import math

import jax
import jax.numpy as jnp
from jax import lax
from jax.experimental import pallas as pl
from jax.experimental.pallas import tpu as pltpu
from jax.sharding import Mesh
from jax.sharding import PartitionSpec as P

BF = jnp.bfloat16
F32 = jnp.float32
GROUP = 4
CTX = ("y", "x", "zh")
HEAD = ("zl", "c")
NN = (((1,), (0,)), ((), ()))
NT = (((1,), (1,)), ((), ()))
TN = (((0,), (0,)), ((), ()))


def dot(a, b, dims=NN):
    return lax.dot_general(a, b, dims, preferred_element_type=F32)


def kernel(
    comp_in, query, d_out, w_uk, w_uv,
    dq_o, dc_o, dw_o,
    comp, wraw, qraw, doraw, tmp, wcat, qh, doh, kvg, lat_t, acc, racc, dqs,
    dwb, r1, r2, e1, r3, r4, f1, r5,
    dcs, c1, s1, c2, s2, c3,
    in_sem, dq_sem, gs_sem, gr_sem, ws_sem, wr_sem, cs_sem, cr_sem,
):
    heads, rows, width = qh.shape
    span, latent = acc.shape
    half_rows = rows // 2
    scale = 1.0 / math.sqrt(width)
    to_exp2 = scale * math.log2(math.e)
    chunks = heads // 2

    y, x, zh = lax.axis_index("y"), lax.axis_index("x"), lax.axis_index("zh")
    zl, core = lax.axis_index("zl"), lax.axis_index("c")
    other = 1 - core
    x_lo = x % 2
    x_pair = x + 1 - 2 * x_lo
    slab = x_lo * 2 + zh
    zpos = zh * 4 + zl

    def remote(src, dst, send, recv, where):
        return pltpu.make_async_remote_copy(
            src_ref=src, dst_ref=dst, send_sem=send, recv_sem=recv,
            device_id=where, device_id_type=pl.DeviceIdType.MESH,
        )

    def z_at(pos):
        return {"zh": pos // 4, "zl": pos % 4}

    loads = [
        pltpu.make_async_copy(w_uk, wraw.at[0], in_sem.at[0]),
        pltpu.make_async_copy(w_uv, wraw.at[1], in_sem.at[1]),
        pltpu.make_async_copy(query, qraw, in_sem.at[2]),
        pltpu.make_async_copy(d_out, doraw, in_sem.at[3]),
        pltpu.make_async_copy(
            comp_in, comp.at[pl.ds(pl.multiple_of(slab * rows, 64), rows)], in_sem.at[4]
        ),
    ]
    for load in loads:
        load.start()

    barrier = pltpu.get_barrier_semaphore()
    peers = [
        {"x": (x + 1) % 4}, {"x": (x + 3) % 4}, {"y": (y + 1) % 4}, {"y": (y + 3) % 4}, {"c": other},
    ] + [z_at((zpos + k) % 8) for k in range(1, 8)]
    for peer in peers:
        pl.semaphore_signal(barrier, inc=1, device_id=peer, device_id_type=pl.DeviceIdType.MESH)
    pl.semaphore_wait(barrier, len(peers))

    def part(which, half):
        return comp.at[pl.ds(pl.multiple_of(which * rows + half * half_rows, 32), half_rows)]

    own = comp_in.at[pl.ds(pl.multiple_of(core * half_rows, 32), half_rows)]
    z_slab = x_lo * 2 + 1 - zh
    x_slab = (1 - x_lo) * 2 + zh
    d_slab = (1 - x_lo) * 2 + 1 - zh

    def z_send(k, target):
        return remote(own, part(slab, core), gs_sem.at[k], gr_sem.at[1], {"zh": 1 - zh, "zl": target})

    x_send = remote(own, part(slab, core), gs_sem.at[0], gr_sem.at[0], {"x": x_pair})
    x_send.start()

    @pl.when(zl == 0)
    def _():
        z_send(1, 3).start()
        z_send(2, 2).start()

    @pl.when(zl == 3)
    def _():
        z_send(1, 0).start()
        z_send(2, 1).start()

    def arrived(which, half, k):
        remote(own, part(which, half), gs_sem.at[0], gr_sem.at[k], {"c": other}).wait_recv()

    def swap(which, k):
        return remote(part(which, core), part(which, core), gs_sem.at[k], gr_sem.at[k], {"c": other})

    diag_send = remote(part(z_slab, core), part(z_slab, core), gs_sem.at[3], gr_sem.at[2], {"x": x_pair})
    swaps = [swap(x_slab, 4), swap(z_slab, 5), swap(d_slab, 6)]

    def relayout_weight(t):
        def step(r, carry):
            at = pl.ds(pl.multiple_of(r * 128, 128), 128)
            tmp[pl.ds(0, 128 * heads), :] = wraw[t, at].reshape(128 * heads, 128).astype(F32)
            for h in range(heads):
                wcat[h, at, t * 128 : (t + 1) * 128] = tmp[pl.ds(h, 128, stride=heads), :].astype(BF)
            return carry

        lax.fori_loop(0, latent // 128, step, 0)

    loads[0].wait()
    relayout_weight(0)
    arrived(x_slab, core, 0)
    swaps[0].start()
    arrived(z_slab, core, 1)
    diag_send.start()
    swaps[1].start()
    loads[1].wait()
    relayout_weight(1)
    arrived(d_slab, core, 2)
    swaps[2].start()
    loads[2].wait()
    loads[3].wait()
    nope = 128
    tmp[...] = qraw[:, :, :nope].reshape(rows * heads, nope).astype(F32)
    for h in range(heads):
        qh[h, :, :nope] = tmp[pl.ds(h, rows, stride=heads), :].astype(BF)
    tmp[:, : width - nope] = qraw[:, :, nope:].reshape(rows * heads, width - nope).astype(F32)
    for h in range(heads):
        qh[h, :, nope:] = tmp[pl.ds(h, rows, stride=heads), :][:, : width - nope].astype(BF)
    tmp[...] = doraw[...].reshape(rows * heads, 128).astype(F32)
    for h in range(heads):
        doh[h] = tmp[pl.ds(h, rows, stride=heads), :].astype(BF)
    loads[4].wait()
    arrived(x_slab, other, 4)
    arrived(z_slab, other, 5)
    arrived(d_slab, other, 6)
    x_send.wait_send()
    diag_send.wait_send()
    for s in swaps:
        s.wait_send()

    @pl.when((zl == 0) | (zl == 3))
    def _():
        z_send(1, 0).wait_send()
        z_send(2, 0).wait_send()

    flipped = comp[:, :latent].T
    lat_t[0] = flipped
    for a in range(4):
        for b in range(4):
            lat_t[1, (b * 4 + a) * 32 : (b * 4 + a + 1) * 32] = flipped[(a * 4 + b) * 32 : (a * 4 + b + 1) * 32]
    acc[...] = jnp.zeros_like(acc)
    racc[...] = jnp.zeros_like(racc)

    def head_pass(h, f):
        e = dot(comp[:, :latent], wcat[h]).astype(BF)
        keys = jnp.concatenate([e[:, :128], comp[:, latent:]], axis=1)
        values = e[:, 128:]
        qq, dd = qh[h], doh[h]
        scores = dot(qq, keys, NT)
        top = jnp.max(scores, axis=1, keepdims=True)
        grown = jnp.exp2((scores - top) * to_exp2)
        probs = grown * (1.0 / jnp.sum(grown, axis=1, keepdims=True))
        grad_probs = dot(dd, values, NT)
        probs_low = probs.astype(BF)
        delta = jnp.sum(probs_low.astype(F32) * grad_probs, axis=1, keepdims=True)
        score_low = (probs * (grad_probs - delta)).astype(BF)
        dqs[h] = dot(score_low, keys) * scale
        pltpu.make_async_copy(dqs.at[h], dq_o.at[h], dq_sem.at[h]).start()
        key_grad = dot(score_low, qq, TN) * scale
        kvg[f, :, :128] = key_grad[:, :128].astype(BF)
        racc[...] += key_grad[:, 128:]
        kvg[f, :, 128:] = dot(probs_low, dd, TN).astype(BF)

    first, second = ("y", "x"), ("x", "y")
    at = {"x": x, "y": y}

    def exchange(k, f, n, axis, to_right, to_left, inbox):
        p = at[axis]
        return [
            remote(to_right, inbox.at[k, f, 0], ws_sem.at[k, f, n], wr_sem.at[k, f, n], {axis: (p + 1) % 4}),
            remote(to_left, inbox.at[k, f, 1], ws_sem.at[k, f, n + 1], wr_sem.at[k, f, n + 1], {axis: (p + 3) % 4}),
        ]

    def spread(k, f, n, axis, buf, inbox, size):
        away = (at[axis] + 2) % 4
        b = buf.at[k, f, away]
        return exchange(k, f, n, axis, b.at[pl.ds(0, size)], b.at[pl.ds(size, size)], inbox)

    def pass_on(k, f, n, axis, buf, inbox):
        p = at[axis]
        return exchange(k, f, n, axis, buf.at[k, f, (p + 1) % 4], buf.at[k, f, (p + 3) % 4], inbox)

    def copies(k, f, stage):
        if stage == 0:
            return spread(k, f, 0, first[f], dwb, r1, 64)
        if stage == 1:
            return pass_on(k, f, 2, first[f], dwb, r2)
        if stage == 2:
            return spread(k, f, 4, second[f], e1, r3, 16)
        if stage == 3:
            return pass_on(k, f, 6, second[f], e1, r4)
        return [remote(f1.at[k, f, 1 - zh], r5.at[k, f], ws_sem.at[k, f, 8], wr_sem.at[k, f, 8], {"zh": 1 - zh})]

    def fold(k, f, axis, buf, inbox, size):
        p = at[axis]
        right, left = (p + 1) % 4, (p + 3) % 4
        buf[k, f, right, :size] = (buf[k, f, right, :size].astype(F32) + inbox[k, f, 0].astype(F32)).astype(BF)
        buf[k, f, left, size:] = (buf[k, f, left, size:].astype(F32) + inbox[k, f, 1].astype(F32)).astype(BF)

    def total(k, f, axis, buf, inbox):
        return buf[k, f, at[axis]].astype(F32) + inbox[k, f, 0].astype(F32) + inbox[k, f, 1].astype(F32)

    def advance(stage, k):
        for f in range(2):
            for c in copies(k, f, stage - 1):
                c.wait_recv()
            if stage == 1:
                fold(k, f, first[f], dwb, r1, 64)
            elif stage == 2:
                e1[k, f] = total(k, f, first[f], dwb, r2).astype(BF).reshape(4, 32, 256)
            elif stage == 3:
                fold(k, f, second[f], e1, r3, 16)
            elif stage == 4:
                f1[k, f] = total(k, f, second[f], e1, r4).astype(BF).reshape(2, 16, 256)
            else:
                dw_o[2 * k + f] = f1[k, f, zh].astype(F32) + r5[k, f].astype(F32)
            if stage < 5:
                for c in copies(k, f, stage):
                    c.start()

    def chunk_step(t, carry):
        for f in range(2):
            head_pass(2 * t + f, f)
        both = dot(kvg[0], wcat[2 * t], NT) + dot(kvg[1], wcat[2 * t + 1], NT)
        acc[...] += both
        for f in range(2):
            dwb[t, f] = dot(lat_t[f], kvg[f]).astype(BF).reshape(4, 128, 256)
        for stage in range(5, 0, -1):
            @pl.when(t >= stage)
            def _():
                advance(stage, t - stage)
        for f in range(2):
            for c in copies(t, f, 0):
                c.start()
        return carry

    lax.fori_loop(0, chunks, chunk_step, 0)

    for b in range(GROUP):
        for s in range(8):
            r0 = (b * 8 + s) * 24
            dcs[s % 2, b // 2, b % 2, s // 2, :, :latent] = acc[r0 : r0 + 24].astype(BF)
            dcs[s % 2, b // 2, b % 2, s // 2, :, latent:] = (racc[r0 : r0 + 24]).astype(BF)
    send1 = remote(dcs.at[other], c1, cs_sem.at[0], cr_sem.at[0], {"c": other})
    send1.start()
    send2 = remote(s1.at[1 - x_lo], c2, cs_sem.at[1], cr_sem.at[1], {"x": x_pair})
    sends3 = [
        remote(s2.at[(zpos + k) % 8], c3.at[k - 1], cs_sem.at[1 + k], cr_sem.at[1 + k], z_at((zpos + k) % 8))
        for k in range(1, 8)
    ]

    def tail(t):
        for stage in range(5, 0, -1):
            if 0 <= t - stage < chunks:
                advance(stage, t - stage)

    send1.wait_recv()
    s1[...] = (dcs[core].astype(F32) + c1[...].astype(F32)).astype(BF)
    send2.start()
    tail(chunks)
    send2.wait_recv()
    s2[...] = (s1[x_lo].astype(F32) + c2[...].astype(F32)).astype(BF).reshape(s2.shape)
    for s in sends3:
        s.start()
    tail(chunks + 1)
    tail(chunks + 2)
    sum3 = s2[zpos].astype(F32)
    for k, s in enumerate(sends3):
        s.wait_recv()
        sum3 += c3[k].astype(F32)
    dc_o[...] = sum3
    tail(chunks + 3)
    tail(chunks + 4)

    send1.wait_send()
    send2.wait_send()
    for s in sends3:
        s.wait_send()

    def drain(k, carry):
        for f in range(2):
            for stage in range(5):
                for c in copies(k, f, stage):
                    c.wait_send()
            h = 2 * k + f
            pltpu.make_async_copy(dqs.at[h], dq_o.at[h], dq_sem.at[h]).wait()
        return carry

    lax.fori_loop(0, chunks, drain, 0)


def per_device(compressed, query, d_output, w_uk, w_uv):
    rows, columns = compressed.shape
    latent, heads, nope = w_uk.shape
    width = query.shape[2]
    span = GROUP * rows
    chunks = heads // 2
    anywhere = pl.BlockSpec(memory_space=pl.ANY)
    vmem = pl.BlockSpec(memory_space=pltpu.VMEM)
    dma = pltpu.SemaphoreType.DMA
    dq, dc, dw = pl.pallas_call(
        kernel,
        out_shape=[
            jax.ShapeDtypeStruct((heads, rows, width), F32),
            jax.ShapeDtypeStruct((24, columns), F32),
            jax.ShapeDtypeStruct((heads, 16, 256), F32),
        ],
        in_specs=[anywhere] * 5,
        out_specs=[anywhere, vmem, vmem],
        scratch_shapes=[
            pltpu.VMEM((span, columns), BF),
            pltpu.VMEM((2, latent, heads, 128), BF),
            pltpu.VMEM((rows, heads, width), BF),
            pltpu.VMEM((rows, heads, 128), BF),
            pltpu.VMEM((rows * heads, 128), F32),
            pltpu.VMEM((heads, latent, 256), BF),
            pltpu.VMEM((heads, rows, width), BF),
            pltpu.VMEM((heads, rows, 128), BF),
            pltpu.VMEM((2, span, 256), BF),
            pltpu.VMEM((2, latent, span), BF),
            pltpu.VMEM((span, latent), F32),
            pltpu.VMEM((span, width - nope), F32),
            pltpu.VMEM((heads, rows, width), F32),
            pltpu.VMEM((chunks, 2, 4, 128, 256), BF),
            pltpu.VMEM((chunks, 2, 2, 64, 256), BF),
            pltpu.VMEM((chunks, 2, 2, 128, 256), BF),
            pltpu.VMEM((chunks, 2, 4, 32, 256), BF),
            pltpu.VMEM((chunks, 2, 2, 16, 256), BF),
            pltpu.VMEM((chunks, 2, 2, 32, 256), BF),
            pltpu.VMEM((chunks, 2, 2, 16, 256), BF),
            pltpu.VMEM((chunks, 2, 16, 256), BF),
            pltpu.VMEM((2, 2, 2, 4, 24, columns), BF),
            pltpu.VMEM((2, 2, 4, 24, columns), BF),
            pltpu.VMEM((2, 2, 4, 24, columns), BF),
            pltpu.VMEM((2, 4, 24, columns), BF),
            pltpu.VMEM((8, 24, columns), BF),
            pltpu.VMEM((7, 24, columns), BF),
            dma((5,)), dma((heads,)), dma((7,)), dma((7,)),
            dma((chunks, 2, 9)), dma((chunks, 2, 9)), dma((9,)), dma((9,)),
        ],
        compiler_params=pltpu.CompilerParams(
            collective_id=0, has_side_effects=True, vmem_limit_bytes=58 * 2**20
        ),
        cost_estimate=pl.CostEstimate(
            flops=14_000_000_000, bytes_accessed=10_000_000, transcendentals=2_400_000
        ),
    )(compressed, query, d_output, w_uk, w_uv)
    d_query = jnp.transpose(dq, (1, 0, 2))
    dw = jnp.transpose(dw, (1, 0, 2))
    return d_query, dc, dw[:, :, :128], dw[:, :, 128:]


def solution(mesh):
    torus = Mesh(mesh.devices.reshape(4, 4, 2, 4, 2), CTX + HEAD)
    return jax.shard_map(
        per_device,
        mesh=torus,
        in_specs=(
            P(CTX, None),
            P(CTX, HEAD, None),
            P(CTX, HEAD, None),
            P(None, HEAD, None),
            P(None, HEAD, None),
        ),
        out_specs=(
            P(CTX, HEAD, None),
            P(CTX + HEAD, None),
            P(CTX, HEAD, None),
            P(CTX, HEAD, None),
        ),
        check_vma=False,
    )
```

time: 209 us -> 97.3 us (0.47)
  Pallas kernels: 0 us -> 88.9 us
  waiting for transfers between devices: 76.7 us -> 0 us
  matrix products: 60.4 us -> 0 us
  local copies, waits for them, and re-layouts: 27.5 us -> 7.46 us
  starting transfers between devices: 19 us -> 0 us
  between operations: 14.1 us -> 0.66 us
  other arithmetic: 9.14 us -> 0 us
    pallas_call x0 -> x1, Pallas kernels: none -> 88.9 us  [per_device(): pl.pallas_call(kernel, out_shape=[jax.ShapeDtypeStruct((heads, rows, widt...]
    reduce_scatter x3 -> x0, waiting for transfers between devices: 63 us -> none  [summed_rows(): total = lax.psum_scatter(total, axis, scatter_dimension=0, tiled=True)]
    dot_general x11 -> x0, matrix products: 49.4 us -> none  [the longest x1 8.22 us: per_device(): lax.dot_general(latent, key_value, (((0,), (0,)), ((), ())), preferred_el...]
    ppermute x4 -> x0, starting transfers between devices: 14.7 us -> none  [partner(): lax.ppermute(value, axis, [(i, i ^ 1 << apart) for i in range(lax.axis_si...]
    ppermute x4 -> x0, waiting for transfers between devices: 13.7 us -> none  [partner(): lax.ppermute(value, axis, [(i, i ^ 1 << apart) for i in range(lax.axis_si...]
    sub x1 -> x0, matrix products: 11 us -> none  [per_device(): probs = jax.nn.softmax(scores, axis=-1)]
    unnamed x40 -> x8, local copies, waits for them, and re-layouts: 18.4 us -> 7.44 us
    concatenate x2 -> x0, local copies, waits for them, and re-layouts: 5.74 us -> none  [the longest x1 3.52 us: per_device(): jnp.concatenate([w_uk.reshape(latent_width, -1), w_uv.reshape(latent_widt...]
  transfers between devices with their start and end apart: 8 -> 0, of which waited for: 5 -> 0; matrix products, arithmetic and copies ran while one was open for 19% -> 0% of each run, Pallas kernels for 0% -> 0%
where the time goes in v1:
time: 97.3 us; the launch traced here: 97 us
  Pallas kernels  88.9 us (91%)
  local copies, waits for them, and re-layouts  7.46 us (8%)
    pallas_call x1, Pallas kernels, per_device(): pl.pallas_call(kernel, out_shape=[jax.ShapeDtypeStruct((heads, rows, widt...  88.9 us
    unnamed x8, local copies, waits for them, and re-layouts  7.44 us

profile of v1, /device:TPU:32, one launch (start us, length us, event | category | flops | bytes accessed | tf_op | source)
XLA Modules:
  0.0 97.0 jit_solution(17817993362617797297)
XLA Ops:
  0.6 88.9 %shard_map.84 = (f32[16,192,192]{2,1,0:T(8,128)}, f32[24,576]{1,0:T(8,128)}, f32[16,16,256]{2,1,0:T(8,128)}) custom-call(bf16[192,576]{1,0:T(8,128)(2,1)} %comp_in.1, bf16[192,16,192]{2,1,0:T(8,128)(2,1)} %query.1, bf16[192,16,128]{2,1,0:T(8,128)(2,1)} %d_out.1, bf16[512,16,128]{2,1,0:T(8,128)(2,1)} %w_uk.1, bf16[512,16,128]{2,1,0:T(8,128)(2,1)} %w_uv.1), custom_call_target="tpu_custom_call" | custom-call | flops 14000000000 | bytes 10000000 | tf_op jit(solution)/shard_map/pallas_call | solution.py:323
  89.5 0.0 copy-start
  89.5 0.0 copy-start.1
  89.5 5.4 %copy.9 = f32[192,16,192]{2,1,0:T(8,128)} copy(f32[192,16,192]{2,0,1:T(8,128)} %bitcast.2) | data formatting | bytes 4718592
  95.0 0.0 copy-done
  95.0 0.7 copy.11
  95.7 0.7 copy.10
  96.4 0.0 copy-done.1
  96.4 0.6 copy.13
  (1 shorter events, 0.0 us)
Async XLA Ops:
  89.5 5.4 %copy-start = (f32[16,16,256]{2,1,0:T(8,128)S(1)}, f32[16,16,256]{2,1,0:T(8,128)}, u32[]{:S(2)}) copy-start(f32[16,16,256]{2,1,0:T(8,128)} %get-tuple-element.9) | copy-start | bytes 786436
  89.5 6.8 %copy-start.1 = (f32[24,576]{1,0:T(8,128)S(1)}, f32[24,576]{1,0:T(8,128)}, u32[]{:S(2)}) copy-start(f32[24,576]{1,0:T(8,128)} %get-tuple-element.21) | copy-start | bytes 165892

commit v2 on v1

v2 whole, which is shorter than its diff:
```python
import functools
import math

import jax
import jax.numpy as jnp
from jax import lax
from jax.experimental import pallas as pl
from jax.experimental.pallas import tpu as pltpu
from jax.sharding import Mesh
from jax.sharding import PartitionSpec as P

BF = jnp.bfloat16
F32 = jnp.float32
GROUP = 4
LAG = (0, 2, 4, 6, 8)
DIRECT = 2
CTX = ("y", "x", "zh")
HEAD = ("zl", "c")
NN = (((1,), (0,)), ((), ()))
NT = (((1,), (1,)), ((), ()))
TN = (((0,), (0,)), ((), ()))


def dot(a, b, dims=NN):
    return lax.dot_general(a, b, dims, preferred_element_type=F32)


def kernel(
    comp_in, query, d_out, w_uk, w_uv,
    dq_o, dc_o, dw_o,
    comp, wraw, qraw, doraw, tmp, wcat, qh, doh, kv, kvg, lat_t, acc, racc, dqs,
    dwb, r1, r2, e1, r3, f1, r4,
    dcs, c1, s1, c2, s2, c3,
    in_sem, gs_sem, gr_sem, ws_sem, wr_sem, cs_sem, cr_sem,
):
    heads, rows, width = qh.shape
    span, latent = acc.shape
    half_rows = rows // 2
    scale = 1.0 / math.sqrt(width)
    to_exp2 = scale * math.log2(math.e)
    chunks = heads // 2

    y, x, zh = lax.axis_index("y"), lax.axis_index("x"), lax.axis_index("zh")
    zl, core = lax.axis_index("zl"), lax.axis_index("c")
    other = 1 - core
    x_lo = x % 2
    x_pair = x + 1 - 2 * x_lo
    slab = x_lo * 2 + zh
    zpos = zh * 4 + zl

    def turn(p, k):
        return (p + k) % 4

    x_other, core_other, zh_other = {"x": x_pair}, {"c": other}, {"zh": 1 - zh}
    z_pos = [(zpos + k) % 8 for k in range(1, 8)]
    z_ring = [{"zh": q // 4, "zl": q % 4} for q in z_pos]

    def remote(src, dst, send, recv, where):
        return pltpu.make_async_remote_copy(
            src_ref=src, dst_ref=dst, send_sem=send, recv_sem=recv,
            device_id=where, device_id_type=pl.DeviceIdType.MESH,
        )

    loads = [
        pltpu.make_async_copy(w_uk, wraw.at[0], in_sem.at[0]),
        pltpu.make_async_copy(w_uv, wraw.at[1], in_sem.at[1]),
        pltpu.make_async_copy(query, qraw, in_sem.at[2]),
        pltpu.make_async_copy(d_out, doraw, in_sem.at[3]),
        pltpu.make_async_copy(
            comp_in, comp.at[pl.ds(pl.multiple_of(slab * rows, 64), rows)], in_sem.at[4]
        ),
    ]
    for load in loads:
        load.start()

    barrier = pltpu.get_barrier_semaphore()
    peers = [{axis: turn(p, k)} for axis, p in (("x", x), ("y", y)) for k in (1, 2, 3)] + [core_other] + z_ring
    for peer in peers:
        pl.semaphore_signal(barrier, inc=1, device_id=peer, device_id_type=pl.DeviceIdType.MESH)

    def relayout_weight(t):
        def step(r, carry):
            at = pl.ds(pl.multiple_of(r * 128, 128), 128)
            tmp[pl.ds(0, 128 * heads), :] = wraw[t, at].reshape(128 * heads, 128).astype(F32)
            for h in range(heads):
                wcat[h, at, t * 128 : (t + 1) * 128] = tmp[pl.ds(h, 128, stride=heads), :].astype(BF)
            return carry

        lax.fori_loop(0, latent // 128, step, 0)

    loads[0].wait()
    relayout_weight(0)
    pl.semaphore_wait(barrier, len(peers))

    def part(which, half):
        return comp.at[pl.ds(pl.multiple_of(which * rows + half * half_rows, 32), half_rows)]

    own = comp_in.at[pl.ds(pl.multiple_of(core * half_rows, 32), half_rows)]
    z_slab = x_lo * 2 + 1 - zh
    x_slab = (1 - x_lo) * 2 + zh
    d_slab = (1 - x_lo) * 2 + 1 - zh

    def z_send(k, target):
        return remote(own, part(slab, core), gs_sem.at[k], gr_sem.at[1], {"zh": 1 - zh, "zl": target})

    x_send = remote(own, part(slab, core), gs_sem.at[0], gr_sem.at[0], x_other)
    x_send.start()

    @pl.when(zl == 0)
    def _():
        z_send(1, 3).start()
        z_send(2, 2).start()

    @pl.when(zl == 3)
    def _():
        z_send(1, 0).start()
        z_send(2, 1).start()

    def arrived(which, half, k):
        remote(own, part(which, half), gs_sem.at[0], gr_sem.at[k], core_other).wait_recv()

    def swap(which, k):
        return remote(part(which, core), part(which, core), gs_sem.at[k], gr_sem.at[k], core_other)

    diag_send = remote(part(z_slab, core), part(z_slab, core), gs_sem.at[3], gr_sem.at[2], x_other)
    swaps = [swap(x_slab, 4), swap(z_slab, 5), swap(d_slab, 6)]

    def expand(which):
        at = pl.ds(pl.multiple_of(which * rows, 64), rows)
        piece = comp[at, :latent]

        def step(h, carry):
            kv[2 * h, at] = dot(piece, wcat[2 * h]).astype(BF)
            kv[2 * h + 1, at] = dot(piece, wcat[2 * h + 1]).astype(BF)
            return carry

        lax.fori_loop(0, heads // 2, step, 0)

    loads[1].wait()
    relayout_weight(1)
    arrived(x_slab, core, 0)
    swaps[0].start()
    loads[2].wait()
    loads[3].wait()
    nope = 128
    tmp[: rows * heads] = qraw[:, :, :nope].reshape(rows * heads, nope).astype(F32)
    for h in range(heads):
        qh[h, :, :nope] = tmp[pl.ds(h, rows, stride=heads), :].astype(BF)
    tmp[: rows * heads, : width - nope] = qraw[:, :, nope:].reshape(rows * heads, width - nope).astype(F32)
    for h in range(heads):
        qh[h, :, nope:] = tmp[pl.ds(h, rows, stride=heads), :][:, : width - nope].astype(BF)
    tmp[: rows * heads] = doraw[...].reshape(rows * heads, 128).astype(F32)
    for h in range(heads):
        doh[h] = tmp[pl.ds(h, rows, stride=heads), :].astype(BF)
    arrived(z_slab, core, 1)
    diag_send.start()
    swaps[1].start()
    loads[4].wait()
    expand(slab)
    arrived(x_slab, other, 4)
    expand(x_slab)
    arrived(d_slab, core, 2)
    swaps[2].start()
    arrived(z_slab, other, 5)
    expand(z_slab)
    acc[...] = jnp.zeros_like(acc)
    racc[...] = jnp.zeros_like(racc)
    arrived(d_slab, other, 6)
    expand(d_slab)
    x_send.wait_send()
    diag_send.wait_send()
    for s in swaps:
        s.wait_send()

    @pl.when((zl == 0) | (zl == 3))
    def _():
        z_send(1, 0).wait_send()
        z_send(2, 0).wait_send()

    flipped = comp[:, :latent].T
    lat_t[0] = flipped
    for a in range(4):
        for b in range(4):
            lat_t[1, (b * 4 + a) * 32 : (b * 4 + a + 1) * 32] = flipped[(a * 4 + b) * 32 : (a * 4 + b + 1) * 32]

    def weigh(h):
        keys = jnp.concatenate([kv[h, :, :128], comp[:, latent:]], axis=1)
        qq, dd = qh[h], doh[h]
        scores = dot(qq, keys, NT)
        grad_probs = dot(dd, kv[h, :, 128:], NT)
        top = jnp.max(scores, axis=1, keepdims=True)
        grown = jnp.exp2((scores - top) * to_exp2)
        probs = grown * (1.0 / jnp.sum(grown, axis=1, keepdims=True))
        probs_low = probs.astype(BF)
        delta = jnp.sum(probs_low.astype(F32) * grad_probs, axis=1, keepdims=True)
        score_low = (probs * (grad_probs - delta)).astype(BF)
        return keys, qq, dd, probs_low, score_low

    def grads(h, f, keys, qq, dd, probs_low, score_low):
        dqs[h] = dot(score_low, keys) * scale
        key_grad = dot(score_low, qq, TN) * scale
        kvg[f, :, :128] = key_grad[:, :128].astype(BF)
        racc[...] += key_grad[:, 128:]
        kvg[f, :, 128:] = dot(probs_low, dd, TN).astype(BF)

    ways = (
        (y, "y", turn(y, 1), turn(y, 3), turn(y, 2)),
        (x, "x", turn(x, 1), turn(x, 3), turn(x, 2)),
    )
    straight = chunks - DIRECT

    def send(k, f, n, src, inbox, where):
        return remote(src, inbox, ws_sem.at[k, f, n], wr_sem.at[k, f, n], where)

    def copies(k, f, stage):
        p, axis, right, left, away = ways[f if stage < 2 else 1 - f]
        right_id, left_id, far_id = {axis: right}, {axis: left}, {axis: away}
        if stage == 0:
            b = dwb.at[k, f, away]
            skip = k // straight
            return [
                send(k, f, 0, b.at[pl.ds(0, 64)], r1.at[k, f, 0], {axis: (p + 1 + skip) % 4}),
                send(k, f, 1, b.at[pl.ds(64, 64)], r1.at[k, f, 1], {axis: (p + 3 - skip) % 4}),
            ]
        if stage == 1:
            return [
                send(k, f, 2, dwb.at[k, f, right], r2.at[k, f, 0], right_id),
                send(k, f, 3, dwb.at[k, f, left], r2.at[k, f, 1], left_id),
            ]
        if stage == 2:
            return [
                send(k, f, 4, e1.at[k, f, away], r3.at[k, f, 2], far_id),
                send(k, f, 5, e1.at[k, f, right], r3.at[k, f, 0], right_id),
                send(k, f, 6, e1.at[k, f, left], r3.at[k, f, 1], left_id),
            ]
        return [send(k, f, 7, f1.at[k, f, 1 - zh], r4.at[k, f], zh_other)]

    def advance(stage, k):
        last = isinstance(k, int) and k >= straight
        for f in range(2):
            for c in copies(k, f, stage - 1):
                c.wait_recv()
            p, _, right, left, _ = ways[f if stage < 3 else 1 - f]
            if stage == 1:
                dwb[k, f, right, :64] = (dwb[k, f, right, :64].astype(F32) + r1[k, f, 0].astype(F32)).astype(BF)
                dwb[k, f, left, 64:] = (dwb[k, f, left, 64:].astype(F32) + r1[k, f, 1].astype(F32)).astype(BF)
            elif stage == 2:
                total = dwb[k, f, p].astype(F32) + r2[k, f, 0].astype(F32) + r2[k, f, 1].astype(F32)
                if last:
                    for c in copies(k, f, 0):
                        c.wait_recv()
                    total += r1[k, f].reshape(128, 256).astype(F32)
                e1[k, f] = total.astype(BF).reshape(4, 32, 256)
            elif stage == 3:
                total = e1[k, f, p].astype(F32)
                for q in range(3):
                    total += r3[k, f, q].astype(F32)
                f1[k, f] = total.astype(BF).reshape(2, 16, 256)
            else:
                dw_o[2 * k + f] = f1[k, f, zh].astype(F32) + r4[k, f].astype(F32)
            if stage < 4:
                for c in copies(k, f, stage):
                    c.start()

    send1 = remote(dcs.at[other], c1, cs_sem.at[0], cr_sem.at[0], core_other)

    def pack_latent():
        for b in range(GROUP):
            for s in range(8):
                r0 = (b * 8 + s) * 24
                dcs[s % 2, (b % 2) * 4 + s // 2, b // 2, :, :latent] = acc[r0 : r0 + 24].astype(BF)
                dcs[s % 2, (b % 2) * 4 + s // 2, b // 2, :, latent:] = racc[r0 : r0 + 24].astype(BF)
        send1.start()

    def chunk_step(t, carry):
        weighed = [weigh(2 * t + f) for f in range(2)]
        for f in range(2):
            grads(2 * t + f, f, *weighed[f])
        both = dot(kvg[0], wcat[2 * t], NT) + dot(kvg[1], wcat[2 * t + 1], NT)
        acc[...] += both
        pl.when(t == chunks - 1)(pack_latent)
        for f in range(2):
            dwb[t, f] = dot(lat_t[f], kvg[f]).astype(BF).reshape(4, 128, 256)
        for f in range(2):
            for c in copies(t, f, 0):
                c.start()

        @pl.when(t >= straight)
        def _():
            for f in range(2):
                for c in copies(t, f, 1):
                    c.start()

        for stage in [q for q in range(1, 5) if LAG[q] < chunks]:
            @pl.when(t >= LAG[stage])
            def _():
                advance(stage, t - LAG[stage])
        return carry

    lax.fori_loop(0, chunks, chunk_step, 0)

    sends2 = [
        remote(s1.at[z_pos[k]], c2.at[k], cs_sem.at[2 + k], cr_sem.at[2 + k], z_ring[k]) for k in range(7)
    ]
    send3 = remote(s2.at[1 - x_lo], c3, cs_sem.at[1], cr_sem.at[1], x_other)

    def tail(t):
        for stage in range(1, 5):
            k = t - LAG[stage]
            if 0 <= k < (straight if stage == 1 else chunks):
                advance(stage, k)

    out_copies = [pltpu.make_async_copy(dqs, dq_o, in_sem.at[0])]
    for c in out_copies:
        c.start()
    send1.wait_recv()
    s1[...] = (dcs[core].astype(F32) + c1[...].astype(F32)).astype(BF)
    for s in sends2:
        s.start()
    for t in range(chunks, chunks + LAG[3]):
        tail(t)
    across = s1[zpos].astype(F32)
    for k, s in enumerate(sends2):
        s.wait_recv()
        across += c2[k].astype(F32)
    s2[...] = across.astype(BF)
    send3.start()
    for t in range(chunks + LAG[3], chunks + LAG[4]):
        tail(t)
    send3.wait_recv()
    dc_o[...] = s2[x_lo].astype(F32) + c3[...].astype(F32)

    for c in out_copies:
        c.wait()
    send1.wait_send()
    send3.wait_send()
    for s in sends2:
        s.wait_send()

    def drain(k, carry):
        for f in range(2):
            for stage in range(4):
                for c in copies(k, f, stage):
                    c.wait_send()
        return carry

    lax.fori_loop(0, chunks, drain, 0)


def per_device(compressed, query, d_output, w_uk, w_uv):
    rows, columns = compressed.shape
    latent, heads, nope = w_uk.shape
    width = query.shape[2]
    span = GROUP * rows
    chunks = heads // 2
    anywhere = pl.BlockSpec(memory_space=pl.ANY)
    vmem = pl.BlockSpec(memory_space=pltpu.VMEM)
    dma = pltpu.SemaphoreType.DMA
    dq, dc, dw = pl.pallas_call(
        kernel,
        out_shape=[
            jax.ShapeDtypeStruct((heads, rows, width), F32),
            jax.ShapeDtypeStruct((24, columns), F32),
            jax.ShapeDtypeStruct((heads, 16, 256), F32),
        ],
        in_specs=[pl.BlockSpec(memory_space=pltpu.HBM)] * 5,
        out_specs=[anywhere, vmem, vmem],
        scratch_shapes=[
            pltpu.VMEM((span, columns), BF),
            pltpu.VMEM((2, latent, heads, 128), BF),
            pltpu.VMEM((rows, heads, width), BF),
            pltpu.VMEM((rows, heads, 128), BF),
            pltpu.VMEM((rows * heads + heads, 128), F32),
            pltpu.VMEM((heads, latent, 256), BF),
            pltpu.VMEM((heads, rows, width), BF),
            pltpu.VMEM((heads, rows, 128), BF),
            pltpu.VMEM((heads, span, 256), BF),
            pltpu.VMEM((2, span, 256), BF),
            pltpu.VMEM((2, latent, span), BF),
            pltpu.VMEM((span, latent), F32),
            pltpu.VMEM((span, width - nope), F32),
            pltpu.VMEM((heads, rows, width), F32),
            pltpu.VMEM((chunks, 2, 4, 128, 256), BF),
            pltpu.VMEM((chunks, 2, 2, 64, 256), BF),
            pltpu.VMEM((chunks, 2, 2, 128, 256), BF),
            pltpu.VMEM((chunks, 2, 4, 32, 256), BF),
            pltpu.VMEM((chunks, 2, 3, 32, 256), BF),
            pltpu.VMEM((chunks, 2, 2, 16, 256), BF),
            pltpu.VMEM((chunks, 2, 16, 256), BF),
            pltpu.VMEM((2, 8, 2, 24, columns), BF),
            pltpu.VMEM((8, 2, 24, columns), BF),
            pltpu.VMEM((8, 2, 24, columns), BF),
            pltpu.VMEM((7, 2, 24, columns), BF),
            pltpu.VMEM((2, 24, columns), BF),
            pltpu.VMEM((24, columns), BF),
            dma((5,)), dma((7,)), dma((7,)),
            dma((chunks, 2, 8)), dma((chunks, 2, 8)), dma((9,)), dma((9,)),
        ],
        compiler_params=pltpu.CompilerParams(
            collective_id=0, has_side_effects=True, vmem_limit_bytes=57 * 2**20
        ),
        cost_estimate=pl.CostEstimate(
            flops=14_000_000_000, bytes_accessed=10_000_000, transcendentals=2_400_000
        ),
    )(compressed, query, d_output, w_uk, w_uv)
    dq = jnp.transpose(dq, (1, 0, 2))
    dw = jnp.transpose(dw, (1, 0, 2))
    return dq, dc, dw[:, :, :128], dw[:, :, 128:]


def solution(mesh):
    torus = Mesh(mesh.devices.reshape(4, 4, 2, 4, 2), CTX + HEAD)
    return jax.shard_map(
        per_device,
        mesh=torus,
        in_specs=(
            P(CTX, None),
            P(CTX, HEAD, None),
            P(CTX, HEAD, None),
            P(None, HEAD, None),
            P(None, HEAD, None),
        ),
        out_specs=(
            P(CTX, HEAD, None),
            P(CTX + HEAD, None),
            P(CTX, HEAD, None),
            P(CTX, HEAD, None),
        ),
        check_vma=False,
    )
```

time: 97.3 us -> 84.2 us (0.87)
  Pallas kernels: 88.9 us -> 76 us
    pallas_call x1, Pallas kernels: 88.9 us -> 76 us  [per_device(): pl.pallas_call(kernel, out_shape=[jax.ShapeDtypeStruct((heads, rows, widt...]
where the time goes in v2:
time: 84.2 us; the launch traced here: 84.1 us
  Pallas kernels  76 us (90%)
  local copies, waits for them, and re-layouts  7.46 us (9%)
    pallas_call x1, Pallas kernels, per_device(): pl.pallas_call(kernel, out_shape=[jax.ShapeDtypeStruct((heads, rows, widt...  76 us
    unnamed x8, local copies, waits for them, and re-layouts  7.44 us

profile of v2, /device:TPU:32, one launch (start us, length us, event | category | flops | bytes accessed | tf_op | source)
XLA Modules:
  0.0 84.1 jit_solution(10715031072334184631)
XLA Ops:
  0.6 76.0 %shard_map.84 = (f32[16,192,192]{2,1,0:T(8,128)}, f32[24,576]{1,0:T(8,128)}, f32[16,16,256]{2,1,0:T(8,128)}) custom-call(bf16[192,576]{1,0:T(8,128)(2,1)} %comp_in.1, bf16[192,16,192]{2,1,0:T(8,128)(2,1)} %query.1, bf16[192,16,128]{2,1,0:T(8,128)(2,1)} %d_out.1, bf16[512,16,128]{2,1,0:T(8,128)(2,1)} %w_uk.1, bf16[512,16,128]{2,1,0:T(8,128)(2,1)} %w_uv.1), custom_call_target="tpu_custom_call" | custom-call | flops 14000000000 | bytes 10000000 | tf_op jit(solution)/shard_map/pallas_call | solution.py:359
  76.7 0.0 copy-start
  76.7 0.0 copy-start.1
  76.7 5.4 %copy.9 = f32[192,16,192]{2,1,0:T(8,128)} copy(f32[192,16,192]{2,0,1:T(8,128)} %bitcast.2) | data formatting | bytes 4718592
  82.1 0.0 copy-done
  82.1 0.7 copy.11
  82.8 0.7 copy.10
  83.5 0.0 copy-done.1
  83.5 0.6 copy.13
  (1 shorter events, 0.0 us)
Async XLA Ops:
  76.7 5.4 %copy-start = (f32[16,16,256]{2,1,0:T(8,128)S(1)}, f32[16,16,256]{2,1,0:T(8,128)}, u32[]{:S(2)}) copy-start(f32[16,16,256]{2,1,0:T(8,128)} %get-tuple-element.9) | copy-start | bytes 786436
  76.7 6.8 %copy-start.1 = (f32[24,576]{1,0:T(8,128)S(1)}, f32[24,576]{1,0:T(8,128)}, u32[]{:S(2)}) copy-start(f32[24,576]{1,0:T(8,128)} %get-tuple-element.21) | copy-start | bytes 165892

commit v3 on v2

--- a/solution.py
+++ b/solution.py
@@ -28,7 +28,7 @@
 def kernel(
     comp_in, query, d_out, w_uk, w_uv,
     dq_o, dc_o, dw_o,
-    comp, wraw, qraw, doraw, tmp, wcat, qh, doh, kv, kvg, lat_t, acc, racc, dqs,
+    comp, wraw, qraw, doraw, tmp, wcat, qh, doh, kv, kvg, lat_t, acc, racc, dqn, dqr,
     dwb, r1, r2, e1, r3, f1, r4,
     dcs, c1, s1, c2, s2, c3,
     in_sem, gs_sem, gr_sem, ws_sem, wr_sem, cs_sem, cr_sem,
@@ -197,7 +197,11 @@
         return keys, qq, dd, probs_low, score_low
 
     def grads(h, f, keys, qq, dd, probs_low, score_low):
-        dqs[h] = dot(score_low, keys) * scale
+        d_q = dot(score_low, keys) * scale
+        dqn[pl.ds(h, rows, stride=heads), :] = d_q[:, :128]
+        dqr[pl.ds(h, rows, stride=heads), :] = jnp.concatenate(
+            [d_q[:, 128:], jnp.zeros((rows, 256 - width), F32)], axis=1
+        )
         key_grad = dot(score_low, qq, TN) * scale
         kvg[f, :, :128] = key_grad[:, :128].astype(BF)
         racc[...] += key_grad[:, 128:]
@@ -210,7 +214,7 @@
     straight = chunks - DIRECT
 
     def send(k, f, n, src, inbox, where):
-        return remote(src, inbox, ws_sem.at[k, f, n], wr_sem.at[k, f, n], where)
+        return remote(src, inbox, ws_sem.at[n], wr_sem.at[k, f, n], where)
 
     def copies(k, f, stage):
         p, axis, right, left, away = ways[f if stage < 2 else 1 - f]
@@ -310,7 +314,10 @@
             if 0 <= k < (straight if stage == 1 else chunks):
                 advance(stage, k)
 
-    out_copies = [pltpu.make_async_copy(dqs, dq_o, in_sem.at[0])]
+    out_copies = [
+        pltpu.make_async_copy(dqn.at[pl.ds(0, rows * heads)], dq_o.at[:, pl.ds(0, 128)], in_sem.at[0]),
+        pltpu.make_async_copy(dqr.at[pl.ds(0, rows * heads)], dq_o.at[:, pl.ds(128, 128)], in_sem.at[1]),
+    ]
     for c in out_copies:
         c.start()
     send1.wait_recv()
@@ -337,14 +344,9 @@
     for s in sends2:
         s.wait_send()
 
-    def drain(k, carry):
-        for f in range(2):
-            for stage in range(4):
-                for c in copies(k, f, stage):
-                    c.wait_send()
-        return carry
-
-    lax.fori_loop(0, chunks, drain, 0)
+    for n, sent in enumerate((r1, r1, r2, r2, r3, r3, r3, r4)):
+        whole = sent.at[:, :, 0] if n < 7 else sent
+        remote(whole, whole, ws_sem.at[n], wr_sem.at[0, 0, n], core_other).wait_send()
 
 
 def per_device(compressed, query, d_output, w_uk, w_uv):
@@ -359,7 +361,7 @@
     dq, dc, dw = pl.pallas_call(
         kernel,
         out_shape=[
-            jax.ShapeDtypeStruct((heads, rows, width), F32),
+            jax.ShapeDtypeStruct((rows * heads, 256), F32),
             jax.ShapeDtypeStruct((24, columns), F32),
             jax.ShapeDtypeStruct((heads, 16, 256), F32),
         ],
@@ -379,7 +381,8 @@
             pltpu.VMEM((2, latent, span), BF),
             pltpu.VMEM((span, latent), F32),
             pltpu.VMEM((span, width - nope), F32),
-            pltpu.VMEM((heads, rows, width), F32),
+            pltpu.VMEM((rows * heads + heads, 128), F32),
+            pltpu.VMEM((rows * heads + heads, 128), F32),
             pltpu.VMEM((chunks, 2, 4, 128, 256), BF),
             pltpu.VMEM((chunks, 2, 2, 64, 256), BF),
             pltpu.VMEM((chunks, 2, 2, 128, 256), BF),
@@ -394,7 +397,7 @@
             pltpu.VMEM((2, 24, columns), BF),
             pltpu.VMEM((24, columns), BF),
             dma((5,)), dma((7,)), dma((7,)),
-            dma((chunks, 2, 8)), dma((chunks, 2, 8)), dma((9,)), dma((9,)),
+            dma((8,)), dma((chunks, 2, 8)), dma((9,)), dma((9,)),
         ],
         compiler_params=pltpu.CompilerParams(
             collective_id=0, has_side_effects=True, vmem_limit_bytes=57 * 2**20
@@ -403,7 +406,7 @@
             flops=14_000_000_000, bytes_accessed=10_000_000, transcendentals=2_400_000
         ),
     )(compressed, query, d_output, w_uk, w_uv)
-    dq = jnp.transpose(dq, (1, 0, 2))
+    dq = dq.reshape(rows, heads, 256)[:, :, :width]
     dw = jnp.transpose(dw, (1, 0, 2))
     return dq, dc, dw[:, :, :128], dw[:, :, 128:]
 

time: 84.2 us -> 83.3 us (0.989)
    unnamed x8 -> x6, local copies, waits for them, and re-layouts: 7.44 us -> 5.89 us
    slice x1, local copies, waits for them, and re-layouts: 0.02 us -> 0.99 us  [per_device(): return (dq, dc, dw[:, :, :128], dw[:, :, 128:])]
where the time goes in v3:
time: 83.3 us; the launch traced here: 83.2 us
  Pallas kernels  75.7 us (91%)
  local copies, waits for them, and re-layouts  6.87 us (8%)
    pallas_call x1, Pallas kernels, per_device(): pl.pallas_call(kernel, out_shape=[jax.ShapeDtypeStruct((rows * heads, 256...  75.7 us
    unnamed x6, local copies, waits for them, and re-layouts  5.89 us

profile of v3, /device:TPU:32, one launch (start us, length us, event | category | flops | bytes accessed | tf_op | source)
XLA Modules:
  0.0 83.2 jit_solution(1102276973734737418)
XLA Ops:
  0.6 75.7 %shard_map.84 = (f32[3072,256]{1,0:T(8,128)}, f32[24,576]{1,0:T(8,128)}, f32[16,16,256]{2,1,0:T(8,128)}) custom-call(bf16[192,576]{1,0:T(8,128)(2,1)} %comp_in.1, bf16[192,16,192]{2,1,0:T(8,128)(2,1)} %query.1, bf16[192,16,128]{2,1,0:T(8,128)(2,1)} %d_out.1, bf16[512,16,128]{2,1,0:T(8,128)(2,1)} %w_uk.1, bf16[512,16,128]{2,1,0:T(8,128)(2,1)} %w_uv.1), custom_call_target="tpu_custom_call" | custom-call | flops 14000000000 | bytes 10000000 | tf_op jit(solution)/shard_map/pallas_call | solution.py:361
  76.4 1.0 %fusion = (f32[16,16,128]{2,0,1:T(8,128)S(1)}, f32[16,16,128]{2,0,1:T(8,128)S(1)}) fusion(f32[16,16,256]{2,0,1:T(8,128)} %bitcast.4), kind=kLoop, calls=%fused_computation | loop fusion | bytes 524288 | tf_op jit(solution)/shard_map/slice | solution.py:411
  77.4 0.7 copy.10
  78.1 0.7 copy.9
  78.8 0.0 copy-start
  78.8 3.9 %copy.13 = f32[192,16,192]{2,1,0:T(8,128)} copy(f32[192,16,192]{2,1,0:T(8,128)} %bitcast.3) | data formatting | bytes 4718592
  82.6 0.0 copy-done
  82.6 0.6 copy.14
Async XLA Ops:
  78.8 3.9 %copy-start = (f32[24,576]{1,0:T(8,128)S(1)}, f32[24,576]{1,0:T(8,128)}, u32[]{:S(2)}) copy-start(f32[24,576]{1,0:T(8,128)} %get-tuple-element.21) | copy-start | bytes 165892

commit v4 on v3

--- a/solution.py
+++ b/solution.py
@@ -12,8 +12,8 @@
 BF = jnp.bfloat16
 F32 = jnp.float32
 GROUP = 4
-LAG = (0, 2, 4, 6, 8)
-DIRECT = 2
+LAG = (0, 9, 2, 4, 6)
+DIRECT = 8
 CTX = ("y", "x", "zh")
 HEAD = ("zl", "c")
 NN = (((1,), (0,)), ((), ()))
@@ -221,7 +221,7 @@
         right_id, left_id, far_id = {axis: right}, {axis: left}, {axis: away}
         if stage == 0:
             b = dwb.at[k, f, away]
-            skip = k // straight
+            skip = 1
             return [
                 send(k, f, 0, b.at[pl.ds(0, 64)], r1.at[k, f, 0], {axis: (p + 1 + skip) % 4}),
                 send(k, f, 1, b.at[pl.ds(64, 64)], r1.at[k, f, 1], {axis: (p + 3 - skip) % 4}),
@@ -240,7 +240,7 @@
         return [send(k, f, 7, f1.at[k, f, 1 - zh], r4.at[k, f], zh_other)]
 
     def advance(stage, k):
-        last = isinstance(k, int) and k >= straight
+        last = True
         for f in range(2):
             for c in copies(k, f, stage - 1):
                 c.wait_recv()

time: 83.3 us -> 82.2 us (0.987)
  Pallas kernels: 75.7 us -> 74.6 us
    pallas_call x1, Pallas kernels: 75.7 us -> 74.6 us  [per_device(): pl.pallas_call(kernel, out_shape=[jax.ShapeDtypeStruct((rows * heads, 256...]
where the time goes in v4:
time: 82.2 us; the launch traced here: 82.1 us
  Pallas kernels  74.6 us (91%)
  local copies, waits for them, and re-layouts  6.87 us (8%)
    pallas_call x1, Pallas kernels, per_device(): pl.pallas_call(kernel, out_shape=[jax.ShapeDtypeStruct((rows * heads, 256...  74.6 us
    unnamed x6, local copies, waits for them, and re-layouts  5.89 us

profile of v4, /device:TPU:32, one launch (start us, length us, event | category | flops | bytes accessed | tf_op | source)
XLA Modules:
  0.0 82.1 jit_solution(14340869459387863269)
XLA Ops:
  0.6 74.6 %shard_map.84 = (f32[3072,256]{1,0:T(8,128)}, f32[24,576]{1,0:T(8,128)}, f32[16,16,256]{2,1,0:T(8,128)}) custom-call(bf16[192,576]{1,0:T(8,128)(2,1)} %comp_in.1, bf16[192,16,192]{2,1,0:T(8,128)(2,1)} %query.1, bf16[192,16,128]{2,1,0:T(8,128)(2,1)} %d_out.1, bf16[512,16,128]{2,1,0:T(8,128)(2,1)} %w_uk.1, bf16[512,16,128]{2,1,0:T(8,128)(2,1)} %w_uv.1), custom_call_target="tpu_custom_call" | custom-call | flops 14000000000 | bytes 10000000 | tf_op jit(solution)/shard_map/pallas_call | solution.py:361
  75.2 1.0 %fusion = (f32[16,16,128]{2,0,1:T(8,128)S(1)}, f32[16,16,128]{2,0,1:T(8,128)S(1)}) fusion(f32[16,16,256]{2,0,1:T(8,128)} %bitcast.4), kind=kLoop, calls=%fused_computation | loop fusion | bytes 524288 | tf_op jit(solution)/shard_map/slice | solution.py:411
  76.2 0.7 copy.10
  76.9 0.7 copy.9
  77.6 0.0 copy-start
  77.6 3.9 %copy.13 = f32[192,16,192]{2,1,0:T(8,128)} copy(f32[192,16,192]{2,1,0:T(8,128)} %bitcast.3) | data formatting | bytes 4718592
  81.5 0.0 copy-done
  81.5 0.6 copy.14
Async XLA Ops:
  77.6 3.9 %copy-start = (f32[24,576]{1,0:T(8,128)S(1)}, f32[24,576]{1,0:T(8,128)}, u32[]{:S(2)}) copy-start(f32[24,576]{1,0:T(8,128)} %get-tuple-element.21) | copy-start | bytes 165892

commit v5 on v4

--- a/solution.py
+++ b/solution.py
@@ -100,41 +100,61 @@
     x_slab = (1 - x_lo) * 2 + zh
     d_slab = (1 - x_lo) * 2 + 1 - zh
 
-    def z_send(k, target):
-        return remote(own, part(slab, core), gs_sem.at[k], gr_sem.at[1], {"zh": 1 - zh, "zl": target})
+    quarter = half_rows // 2
+
+    def own_piece(s):
+        return comp_in.at[pl.ds(pl.multiple_of(core * half_rows + s * quarter, 16), quarter)]
+
+    def piece(which, half, s):
+        return comp.at[pl.ds(pl.multiple_of(which * rows + half * half_rows + s * quarter, 16), quarter)]
+
+    def z_send(k, s, target):
+        where = {"zh": 1 - zh, "zl": target}
+        return remote(own_piece(s), piece(slab, core, s), gs_sem.at[1 + 2 * k + s], gr_sem.at[1 + s], where)
 
     x_send = remote(own, part(slab, core), gs_sem.at[0], gr_sem.at[0], x_other)
     x_send.start()
 
     @pl.when(zl == 0)
     def _():
-        z_send(1, 3).start()
-        z_send(2, 2).start()
+        for s in range(2):
+            z_send(0, s, 3).start()
+            z_send(1, s, 2).start()
 
     @pl.when(zl == 3)
     def _():
-        z_send(1, 0).start()
-        z_send(2, 1).start()
+        for s in range(2):
+            z_send(0, s, 0).start()
+            z_send(1, s, 1).start()
 
     def arrived(which, half, k):
         remote(own, part(which, half), gs_sem.at[0], gr_sem.at[k], core_other).wait_recv()
 
+    def piece_arrived(which, half, s, k):
+        remote(own_piece(0), piece(which, half, s), gs_sem.at[0], gr_sem.at[k], core_other).wait_recv()
+
     def swap(which, k):
         return remote(part(which, core), part(which, core), gs_sem.at[k], gr_sem.at[k], core_other)
 
-    diag_send = remote(part(z_slab, core), part(z_slab, core), gs_sem.at[3], gr_sem.at[2], x_other)
-    swaps = [swap(x_slab, 4), swap(z_slab, 5), swap(d_slab, 6)]
-
-    def expand(which):
+    diag_sends = [
+        remote(piece(z_slab, core, s), piece(z_slab, core, s), gs_sem.at[5 + s], gr_sem.at[3 + s], x_other)
+        for s in range(2)
+    ]
+    swaps = [swap(x_slab, 7), swap(z_slab, 8)] + [
+        remote(piece(d_slab, core, s), piece(d_slab, core, s), gs_sem.at[9 + s], gr_sem.at[9 + s], core_other)
+        for s in range(2)
+    ]
+
+    def expand(which, first, last):
         at = pl.ds(pl.multiple_of(which * rows, 64), rows)
-        piece = comp[at, :latent]
+        piece_rows = comp[at, :latent]
 
         def step(h, carry):
-            kv[2 * h, at] = dot(piece, wcat[2 * h]).astype(BF)
-            kv[2 * h + 1, at] = dot(piece, wcat[2 * h + 1]).astype(BF)
+            kv[2 * h, at] = dot(piece_rows, wcat[2 * h]).astype(BF)
+            kv[2 * h + 1, at] = dot(piece_rows, wcat[2 * h + 1]).astype(BF)
             return carry
 
-        lax.fori_loop(0, heads // 2, step, 0)
+        lax.fori_loop(first // 2, last // 2, step, 0)
 
     loads[1].wait()
     relayout_weight(1)
@@ -152,30 +172,36 @@
     tmp[: rows * heads] = doraw[...].reshape(rows * heads, 128).astype(F32)
     for h in range(heads):
         doh[h] = tmp[pl.ds(h, rows, stride=heads), :].astype(BF)
-    arrived(z_slab, core, 1)
-    diag_send.start()
+    piece_arrived(z_slab, core, 0, 1)
+    diag_sends[0].start()
+    loads[4].wait()
+    expand(slab, 0, heads)
+    piece_arrived(z_slab, core, 1, 2)
+    diag_sends[1].start()
     swaps[1].start()
-    loads[4].wait()
-    expand(slab)
-    arrived(x_slab, other, 4)
-    expand(x_slab)
-    arrived(d_slab, core, 2)
+    arrived(x_slab, other, 7)
+    expand(x_slab, 0, heads)
+    piece_arrived(d_slab, core, 0, 3)
     swaps[2].start()
-    arrived(z_slab, other, 5)
-    expand(z_slab)
+    arrived(z_slab, other, 8)
+    expand(z_slab, 0, heads // 2)
+    piece_arrived(d_slab, core, 1, 4)
+    swaps[3].start()
+    expand(z_slab, heads // 2, heads)
     acc[...] = jnp.zeros_like(acc)
     racc[...] = jnp.zeros_like(racc)
-    arrived(d_slab, other, 6)
-    expand(d_slab)
+    piece_arrived(d_slab, other, 0, 9)
+    piece_arrived(d_slab, other, 1, 10)
+    expand(d_slab, 0, heads)
     x_send.wait_send()
-    diag_send.wait_send()
-    for s in swaps:
+    for s in diag_sends + swaps:
         s.wait_send()
 
     @pl.when((zl == 0) | (zl == 3))
     def _():
-        z_send(1, 0).wait_send()
-        z_send(2, 0).wait_send()
+        for s in range(2):
+            z_send(0, s, 0).wait_send()
+            z_send(1, s, 0).wait_send()
 
     flipped = comp[:, :latent].T
     lat_t[0] = flipped
@@ -396,7 +422,7 @@
             pltpu.VMEM((7, 2, 24, columns), BF),
             pltpu.VMEM((2, 24, columns), BF),
             pltpu.VMEM((24, columns), BF),
-            dma((5,)), dma((7,)), dma((7,)),
+            dma((5,)), dma((11,)), dma((11,)),
             dma((8,)), dma((chunks, 2, 8)), dma((9,)), dma((9,)),
         ],
         compiler_params=pltpu.CompilerParams(

time: 82.2 us -> 81 us (0.985)
  Pallas kernels: 74.6 us -> 73.1 us
    pallas_call x1, Pallas kernels: 74.6 us -> 73.1 us  [per_device(): pl.pallas_call(kernel, out_shape=[jax.ShapeDtypeStruct((rows * heads, 256...]
where the time goes in v5:
time: 81 us; the launch traced here: 80.6 us
  Pallas kernels  73.1 us (90%)
  local copies, waits for them, and re-layouts  6.87 us (8%)
    pallas_call x1, Pallas kernels, per_device(): pl.pallas_call(kernel, out_shape=[jax.ShapeDtypeStruct((rows * heads, 256...  73.1 us
    unnamed x6, local copies, waits for them, and re-layouts  5.89 us

profile of v5, /device:TPU:32, one launch (start us, length us, event | category | flops | bytes accessed | tf_op | source)
XLA Modules:
  0.0 80.6 jit_solution(13424183767388963858)
XLA Ops:
  0.6 73.1 %shard_map.84 = (f32[3072,256]{1,0:T(8,128)}, f32[24,576]{1,0:T(8,128)}, f32[16,16,256]{2,1,0:T(8,128)}) custom-call(bf16[192,576]{1,0:T(8,128)(2,1)} %comp_in.1, bf16[192,16,192]{2,1,0:T(8,128)(2,1)} %query.1, bf16[192,16,128]{2,1,0:T(8,128)(2,1)} %d_out.1, bf16[512,16,128]{2,1,0:T(8,128)(2,1)} %w_uk.1, bf16[512,16,128]{2,1,0:T(8,128)(2,1)} %w_uv.1), custom_call_target="tpu_custom_call" | custom-call | flops 14000000000 | bytes 10000000 | tf_op jit(solution)/shard_map/pallas_call | solution.py:387
  73.7 1.0 %fusion = (f32[16,16,128]{2,0,1:T(8,128)S(1)}, f32[16,16,128]{2,0,1:T(8,128)S(1)}) fusion(f32[16,16,256]{2,0,1:T(8,128)} %bitcast.4), kind=kLoop, calls=%fused_computation | loop fusion | bytes 524288 | tf_op jit(solution)/shard_map/slice | solution.py:437
  74.7 0.7 copy.10
  75.4 0.7 copy.9
  76.1 0.0 copy-start
  76.1 3.9 %copy.13 = f32[192,16,192]{2,1,0:T(8,128)} copy(f32[192,16,192]{2,1,0:T(8,128)} %bitcast.3) | data formatting | bytes 4718592
  80.0 0.0 copy-done
  80.0 0.6 copy.14
Async XLA Ops:
  76.1 3.9 %copy-start = (f32[24,576]{1,0:T(8,128)S(1)}, f32[24,576]{1,0:T(8,128)}, u32[]{:S(2)}) copy-start(f32[24,576]{1,0:T(8,128)} %get-tuple-element.21) | copy-start | bytes 165892
